TPU v7x, 32 devices: a whole 2x2x4 slice. The times are simulated.
32 devices in a mesh: leaf: 32 (over z, y, x, core).
Axes of the slice: x: 2, y: 2, z: 4, core: 2. Of those that a mesh axis runs over, the one named last changes fastest.
Arguments:
- charges: bfloat16 [256, 16, 256], P('leaf'), may hold values from -6 to 6
- points: bfloat16 [256, 3, 256], P('leaf'), may hold values from 0 to 2
- near_list: int32 [256, 16], P('leaf'), may hold values from 0 to 255, as said below
- leaf_basis: bfloat16 [256, 64, 256], P('leaf'), may hold values from -0.375 to 0.375
- transfer: bfloat16 [448, 64, 64], P('leaf'), may hold values from -0.625 to 0.625
- coupling: bfloat16 [480, 64, 512], P('leaf'), may hold values from -0.25 to 0.25
- far_list: int32 [480, 8], P('leaf'), may hold values from 0 to 255, as said below
- top_transfer: bfloat16 [2, 64, 64], replicated, may hold values from -0.625 to 0.625
- top_coupling: bfloat16 [4, 64, 64], replicated, may hold values from -0.5 to 0.5
- top_list: int32 [28, 2], replicated, may hold values from 0 to 15, as said below
Outputs:
- potential: float32 [256, 16, 256], P('leaf')
Inputs may be any that keep to these rules, and one draw needn't show every extreme that they name: `near_list`: every entry of the row of leaf g names a leaf within 8 of g; slot 0 is g itself; slot 1 is g + 8, or g - 8 where g + 8 is not a leaf. `far_list`: an entry of the row of node i of block d at level l names a node of level l that belongs to block d - 1, d or d + 1, never node i of block d itself. `top_list`: an entry for node m of a coarse level names a node of the same level whose index differs from m by 1 or 2.
All inputs are finite; a program needn't handle non-finite values.
Results may differ from a plain program's by a relative error of at most 0.012.
Values may be sent and summed in bfloat16 or wider, within the bound.
A program may use at most 64 MiB of HBM per device.

v0:
```python
import jax
import jax.numpy as jnp
from jax import lax
from jax.sharding import PartitionSpec as P

REACH = 8


KERNEL_SCALE = 0.01
SOFTENING = 0.05
PRECISE = lax.Precision.HIGHEST
OFFSETS = (-2, -1, 1, 2)


def with_halo(value, sides, width):
    for axis, dim in sides:
        devices, length = (lax.axis_size(axis), value.shape[dim])
        up = [(i, (i + 1) % devices) for i in range(devices - 1)]
        down = [(j, i) for i, j in up]
        last = lax.slice_in_dim(value, length - width, length, axis=dim)
        first = lax.slice_in_dim(value, 0, width, axis=dim)
        before = lax.ppermute(last, axis, up)
        after = lax.ppermute(first, axis, down)
        value = jnp.concatenate([before, value, after], axis=dim)
    return value


def kernel_tile(targets, sources):
    delta_x = targets[:, None, 0, :, None] - sources[:, :, 0, None, :]
    delta_y = targets[:, None, 1, :, None] - sources[:, :, 1, None, :]
    delta_z = targets[:, None, 2, :, None] - sources[:, :, 2, None, :]
    squared = delta_x * delta_x + delta_y * delta_y + delta_z * delta_z
    return (KERNEL_SCALE * lax.rsqrt(squared + SOFTENING * SOFTENING)).astype(jnp.bfloat16)


def near_field(charges, points, near_list):
    leaf_count, nrhs_count, point_count = charges.shape
    near_count = near_list.shape[1]
    stacked = jnp.concatenate([charges, points], axis=1)
    padded = with_halo(stacked, (("leaf", 0),), REACH)
    first_leaf = lax.axis_index("leaf") * leaf_count - REACH
    fetched = padded[near_list - first_leaf]
    group_size = min(2, leaf_count)
    own_points = points.reshape(leaf_count // group_size, group_size, 3, point_count)
    grouped = fetched.reshape(
        leaf_count // group_size, group_size, near_count, nrhs_count + 3, point_count
    )

    def one_block(pieces):
        targets, sources = pieces
        kernel_vals = kernel_tile(
            targets.astype(jnp.float32), sources[:, :, nrhs_count:, :].astype(jnp.float32)
        )
        return jnp.einsum(
            "gsrb,gsab->gra",
            sources[:, :, :nrhs_count, :],
            kernel_vals,
            preferred_element_type=jnp.float32,
        )

    blocks = lax.map(one_block, (own_points, grouped))
    return blocks.reshape(leaf_count, nrhs_count, point_count)


def couple_nodes(fetched, matrices, nrhs_count, rank_count):
    node_count = fetched.shape[0]
    far_count = fetched.shape[1]
    grouped = fetched.reshape(node_count, far_count, nrhs_count, rank_count)
    weights = matrices.reshape(node_count, rank_count, far_count, rank_count)
    return jnp.einsum("msrq,mksq->mrk", grouped, weights, preferred_element_type=jnp.float32)


def lift(left_child, right_child, top_transfer):
    summed = jnp.einsum(
        "...rk,kj->...rj", left_child, top_transfer[0], preferred_element_type=jnp.float32
    )
    summed = summed + jnp.einsum(
        "...rk,kj->...rj", right_child, top_transfer[1], preferred_element_type=jnp.float32
    )
    return summed.astype(jnp.bfloat16)


def spread(running, matrix):
    return jnp.einsum("...rj,kj->...rk", running, matrix.astype(jnp.float32), precision=PRECISE)


def expand(running, top_transfer):
    left_child = spread(running, top_transfer[0])
    right_child = spread(running, top_transfer[1])
    return jnp.stack([left_child, right_child], axis=1).reshape(
        2 * running.shape[0], running.shape[1], running.shape[2]
    )


def offset_weights(partner_rows, node_ids):
    distance = partner_rows - node_ids[..., None]
    return jnp.stack(
        [jnp.sum((distance == step_off).astype(jnp.int32), axis=-1) for step_off in OFFSETS]
    ).astype(jnp.bfloat16)


def cross_terms(selected, weights, top_coupling):
    scaled = selected * weights[..., None, None]
    return jnp.einsum("o...rk,okj->...rj", scaled, top_coupling, preferred_element_type=jnp.float32)


def gather_roots(block_root, top_transfer, levels_up):
    nrhs_count, rank_count = block_root.shape
    gathered = lax.all_gather(
        block_root.reshape(1, nrhs_count * rank_count), "leaf", axis=0, tiled=True
    )
    upward = [gathered.reshape(gathered.shape[0], nrhs_count, rank_count)]
    for coarse in range(levels_up):
        children = upward[-1]
        upward.append(lift(children[0::2], children[1::2], top_transfer))
    return upward


def coarse_all(upward, top_transfer, top_coupling, top_list, device, total_size, levels_up):
    crossing = []
    for coarse in range(1, levels_up + 1):
        node_count = total_size >> coarse
        start = total_size - 2 * node_count
        partner_rows = top_list[start : start + node_count]
        node_ids = jnp.arange(node_count, dtype=jnp.int32)
        weights = offset_weights(partner_rows, node_ids)
        selected = jnp.stack(
            [
                upward[coarse][jnp.clip(node_ids + step_off, 0, node_count - 1)]
                for step_off in OFFSETS
            ]
        )
        crossing.append(cross_terms(selected, weights, top_coupling))
    running = crossing[-1]
    for coarse in range(levels_up - 1, 0, -1):
        running = crossing[coarse - 1] + expand(running, top_transfer)
    every_root = expand(running, top_transfer)
    return lax.dynamic_index_in_dim(every_root, device, 0, keepdims=False)


def shards(
    charges,
    points,
    near_list,
    leaf_basis,
    transfer,
    coupling,
    far_list,
    top_transfer,
    top_coupling,
    top_list,
):
    near_part = near_field(charges, points, near_list)
    leaf_count = charges.shape[0]
    nrhs_count = charges.shape[1]
    rank_count = leaf_basis.shape[1]
    tree_depth = leaf_count.bit_length() - 1
    device = lax.axis_index("leaf")
    total_size = lax.axis_size("leaf")
    levels_up = total_size.bit_length() - 3
    starts = [2 * leaf_count - 2 * (leaf_count >> height) for height in range(tree_depth + 1)]
    levels = [
        jnp.einsum("lrp,lkp->lrk", charges, leaf_basis, preferred_element_type=jnp.float32).astype(
            jnp.bfloat16
        )
    ]
    for height in range(tree_depth):
        node_count = leaf_count >> height
        lifted = jnp.einsum(
            "crk,ckj->crj",
            levels[-1],
            transfer[starts[height] : starts[height] + node_count],
            preferred_element_type=jnp.float32,
        )
        levels.append((lifted[0::2] + lifted[1::2]).astype(jnp.bfloat16))
    flattened = [tier.reshape(tier.shape[0], nrhs_count * rank_count) for tier in levels]
    coupled = []
    for height in range(tree_depth + 1):
        node_count = leaf_count >> height
        padded = with_halo(flattened[height], (("leaf", 0),), node_count)
        partner_rows = far_list[starts[height] : starts[height] + node_count]
        located = partner_rows - (device - 1) * node_count
        coupled.append(
            couple_nodes(
                padded[located],
                coupling[starts[height] : starts[height] + node_count],
                nrhs_count,
                rank_count,
            )
        )
    block_root = levels[tree_depth].reshape(nrhs_count, rank_count)
    upward = gather_roots(block_root, top_transfer, levels_up)
    descent = coarse_all(
        upward, top_transfer, top_coupling, top_list, device, total_size, levels_up
    )
    running = coupled[tree_depth] + descent[None]
    for height in range(tree_depth - 1, -1, -1):
        node_count = leaf_count >> height
        parent = jnp.repeat(running, 2, axis=0)
        matrices = transfer[starts[height] : starts[height] + node_count].astype(jnp.float32)
        running = coupled[height] + jnp.einsum("crj,ckj->crk", parent, matrices, precision=PRECISE)
    far_part = jnp.einsum(
        "lrk,lkp->lrp", running, leaf_basis.astype(jnp.float32), precision=PRECISE
    )
    return near_part + far_part


def solution(mesh):
    placed = (
        P("leaf", None, None),
        P("leaf", None, None),
        P("leaf", None),
        P("leaf", None, None),
        P("leaf", None, None),
        P("leaf", None, None),
        P("leaf", None),
        P(),
        P(),
        P(),
    )
    return jax.shard_map(
        shards, mesh=mesh, in_specs=placed, out_specs=P("leaf", None, None), check_vma=False
    )
```

profile of v0, /device:TPU:1, one launch (start us, length us, event | category | flops | bytes accessed | tf_op | source)
XLA Modules:
  0.0 116.5 jit_solution(15853237495840425527)
XLA Ops:
  0.0 0.9 constant_dynamic-update-slice_fusion
  0.9 0.7 copy_dynamic-update-slice_fusion
  1.6 2.0 %collective-permute-start.1 = (bf16[8,19,256]{2,1,0:T(8,128)(2,1)S(1)}, bf16[8,19,256]{2,1,0:T(8,128)(2,1)S(1)}, u32[]{:S(2)}, u32[]{:S(2)}) collective-permute-start(bf16[8,19,256]{2,1,0:T(8,128)(2,1)S(1)} %copy_dynamic-update-slice_fusion), channel_id=1, source_target_pairs={{1,0},{2,1},{3,2},{4,3},{5,4},{6,5},{7,6},{8,7},{9,8},{10,9},{11,1... | collective-permute-start | bytes 233480 | tf_op jit(solution)/shard_map/ppermute | solution.py:23
  3.6 4.5 %collective-permute-start = (bf16[8,19,256]{2,1,0:T(8,128)(2,1)S(1)}, bf16[8,19,256]{2,1,0:T(8,128)(2,1)S(1)}, u32[]{:S(2)}, u32[]{:S(2)}) collective-permute-start(bf16[8,19,256]{2,1,0:T(8,128)(2,1)S(1)} %copy_dynamic-update-slice_fusion), channel_id=1, source_target_pairs={{0,1},{1,2},{2,3},{3,4},{4,5},{5,6},{6,7},{7,8},{8,9},{9,10},{10,1... | collective-permute-start | bytes 233480 | tf_op jit(solution)/shard_map/ppermute | solution.py:22
  8.1 1.0 convolution_convert_fusion
  9.1 1.1 fusion.31
  10.2 1.0 fusion.47
  11.2 0.9 fusion.54
  12.1 0.7 reshape.428
  12.7 1.9 %collective-permute-start.9 = (bf16[1,1024]{1,0:T(2,128)(2,1)}, bf16[1,1024]{1,0:T(2,128)(2,1)}, u32[]{:S(2)}, u32[]{:S(2)}) collective-permute-start(bf16[1,1024]{1,0:T(2,128)(2,1)} %reshape.428), channel_id=1, source_target_pairs={{1,0},{2,1},{3,2},{4,3},{5,4},{6,5},{7,6},{8,7},{9,8},{10,9},{11,1... | collective-permute-start | bytes 6152 | tf_op jit(solution)/shard_map/ppermute | solution.py:23
  14.7 3.6 %collective-permute-start.8 = (bf16[1,1024]{1,0:T(2,128)(2,1)}, bf16[1,1024]{1,0:T(2,128)(2,1)}, u32[]{:S(2)}, u32[]{:S(2)}) collective-permute-start(bf16[1,1024]{1,0:T(2,128)(2,1)} %reshape.428), channel_id=1, source_target_pairs={{0,1},{1,2},{2,3},{3,4},{4,5},{5,6},{6,7},{7,8},{8,9},{9,10},{10,1... | collective-permute-start | bytes 6152 | tf_op jit(solution)/shard_map/ppermute | solution.py:22
  18.3 0.7 reshape.425
  19.0 1.9 %collective-permute-start.7 = (bf16[2,1024]{1,0:T(2,128)(2,1)}, bf16[2,1024]{1,0:T(2,128)(2,1)}, u32[]{:S(2)}, u32[]{:S(2)}) collective-permute-start(bf16[2,1024]{1,0:T(2,128)(2,1)} %reshape.425), channel_id=1, source_target_pairs={{1,0},{2,1},{3,2},{4,3},{5,4},{6,5},{7,6},{8,7},{9,8},{10,9},{11,1... | collective-permute-start | bytes 12296 | tf_op jit(solution)/shard_map/ppermute | solution.py:23
  21.0 42.6 %all-gather = bf16[32,1,1024]{2,1,0:T(2,128)(2,1)S(1)} all-gather(bf16[1,1,1024]{2,1,0:T(2,128)(2,1)S(1)} %reshape.589), channel_id=1, replica_groups=mesh['leaf'=32] {'leaf'}, dimensions={0}, use_global_device_ids=true | all-gather | bytes 67584 | tf_op jit(solution)/shard_map/all_gather | solution.py:109
  77.4 0.7 reshape.422
  79.7 1.9 %collective-permute-start.6 = (bf16[2,1024]{1,0:T(2,128)(2,1)}, bf16[2,1024]{1,0:T(2,128)(2,1)S(1)}, u32[]{:S(2)}, u32[]{:S(2)}) collective-permute-start(bf16[2,1024]{1,0:T(2,128)(2,1)} %reshape.425), channel_id=1, source_target_pairs={{0,1},{1,2},{2,3},{3,4},{4,5},{5,6},{6,7},{7,8},{8,9},{9,10},{10,1... | collective-permute-start | bytes 12296 | tf_op jit(solution)/shard_map/ppermute | solution.py:22
  81.6 2.4 %collective-permute-start.5 = (bf16[4,1024]{1,0:T(4,128)(2,1)}, bf16[4,1024]{1,0:T(4,128)(2,1)S(1)}, u32[]{:S(2)}, u32[]{:S(2)}) collective-permute-start(bf16[4,1024]{1,0:T(4,128)(2,1)} %reshape.422), channel_id=1, source_target_pairs={{1,0},{2,1},{3,2},{4,3},{5,4},{6,5},{7,6},{8,7},{9,8},{10,9},{11,1... | collective-permute-start | bytes 24584 | tf_op jit(solution)/shard_map/ppermute | solution.py:23
  84.0 0.7 pad_maximum_fusion.7
  85.6 3.2 %collective-permute-start.4 = (bf16[4,1024]{1,0:T(4,128)(2,1)}, bf16[4,1024]{1,0:T(4,128)(2,1)S(1)}, u32[]{:S(2)}, u32[]{:S(2)}) collective-permute-start(bf16[4,1024]{1,0:T(4,128)(2,1)} %reshape.422), channel_id=1, source_target_pairs={{0,1},{1,2},{2,3},{3,4},{4,5},{5,6},{6,7},{7,8},{8,9},{9,10},{10,1... | collective-permute-start | bytes 24584 | tf_op jit(solution)/shard_map/ppermute | solution.py:22
  88.7 1.9 %collective-permute-start.3 = (bf16[8,1024]{1,0:T(8,128)(2,1)S(1)}, bf16[8,1024]{1,0:T(8,128)(2,1)S(1)}, u32[]{:S(2)}, u32[]{:S(2)}) collective-permute-start(bf16[8,1024]{1,0:T(8,128)(2,1)S(1)} %reshape.419), channel_id=1, source_target_pairs={{1,0},{2,1},{3,2},{4,3},{5,4},{6,5},{7,6},{8,7},{9,8},{10,9},{11,1... | collective-permute-start | bytes 49160 | tf_op jit(solution)/shard_map/ppermute | solution.py:23
  90.7 0.7 pad_maximum_fusion.6
  91.4 0.7 gather_fusion.3
  92.5 3.7 %collective-permute-start.2 = (bf16[8,1024]{1,0:T(8,128)(2,1)S(1)}, bf16[8,1024]{1,0:T(8,128)(2,1)S(1)}, u32[]{:S(2)}, u32[]{:S(2)}) collective-permute-start(bf16[8,1024]{1,0:T(8,128)(2,1)S(1)} %reshape.419), channel_id=1, source_target_pairs={{0,1},{1,2},{2,3},{3,4},{4,5},{5,6},{6,7},{7,8},{8,9},{9,10},{10,1... | collective-permute-start | bytes 49160 | tf_op jit(solution)/shard_map/ppermute | solution.py:22
  96.2 0.7 pad_maximum_fusion.5
  96.9 0.8 gather_fusion.2
  98.4 0.7 gather_fusion.1
  100.7 14.9 %while.10 = (s32[]{:T(128)}, f32[4,2,16,256]{3,2,1,0:T(8,128)S(1)}, bf16[4,2,16,19,256]{4,3,2,1,0:T(8,128)(2,1)S(1)}, bf16[4,2,3,256]{3,1,0,2:T(2,128)(2,1)S(1)}, s32[]{:T(128)}) while((s32[]{:T(128)}, f32[4,2,16,256]{3,2,1,0:T(8,128)S(1)}, bf16[4,2,16,19,256]{4,3,2,1,0:T(8,128)(2,1)S(1)}, bf16[4,2,3,256]{3,1,0,2:T(2,128)(2,1)S(1)}, ...), condition=%wide.region_1.2_spmd, body=%wide.region_0.1_spmd.sunk | while | flops 90203648 | bytes 1584209 | solution.py:61
  100.9 3.5 %fusion.138 = f32[4,2,16,256]{3,2,1,0:T(8,128)S(1)} fusion(f32[4,2,16,256]{3,2,1,0:T(8,128)S(1)} %get-tuple-element.139, s32[]{:T(128)S(6)} %copy.89, f32[2,16,256]{2,1,0:T(8,128)S(1)} %get-tuple-element.127, f32[2,256]{1,0:T(2,128)S(1)} %get-tuple-element.128, f32[2,16,256]{2,1,0:T(8,128)S(1)} %get-tuple-element.129, ...), kind=kOutput, calls=%fused_computation.20.clone.1 | convolution fusion | flops 90177536 | bytes 399364 | tf_op jit(solution)/shard_map/while/body/eval_jaxpr/gsrb,gsab->gra/dot_general | solution.py:54
  104.6 3.5 %fusion.138 = f32[4,2,16,256]{3,2,1,0:T(8,128)S(1)} fusion(f32[4,2,16,256]{3,2,1,0:T(8,128)S(1)} %get-tuple-element.139, s32[]{:T(128)S(6)} %copy.89, f32[2,16,256]{2,1,0:T(8,128)S(1)} %get-tuple-element.127, f32[2,256]{1,0:T(2,128)S(1)} %get-tuple-element.128, f32[2,16,256]{2,1,0:T(8,128)S(1)} %get-tuple-element.129, ...), kind=kOutput, calls=%fused_computation.20.clone.1 | convolution fusion | flops 90177536 | bytes 399364 | tf_op jit(solution)/shard_map/while/body/eval_jaxpr/gsrb,gsab->gra/dot_general | solution.py:54
  108.4 3.5 %fusion.138 = f32[4,2,16,256]{3,2,1,0:T(8,128)S(1)} fusion(f32[4,2,16,256]{3,2,1,0:T(8,128)S(1)} %get-tuple-element.139, s32[]{:T(128)S(6)} %copy.89, f32[2,16,256]{2,1,0:T(8,128)S(1)} %get-tuple-element.127, f32[2,256]{1,0:T(2,128)S(1)} %get-tuple-element.128, f32[2,16,256]{2,1,0:T(8,128)S(1)} %get-tuple-element.129, ...), kind=kOutput, calls=%fused_computation.20.clone.1 | convolution fusion | flops 90177536 | bytes 399364 | tf_op jit(solution)/shard_map/while/body/eval_jaxpr/gsrb,gsab->gra/dot_general | solution.py:54
  112.1 3.5 %fusion.138 = f32[4,2,16,256]{3,2,1,0:T(8,128)S(1)} fusion(f32[4,2,16,256]{3,2,1,0:T(8,128)S(1)} %get-tuple-element.139, s32[]{:T(128)S(6)} %copy.89, f32[2,16,256]{2,1,0:T(8,128)S(1)} %get-tuple-element.127, f32[2,256]{1,0:T(2,128)S(1)} %get-tuple-element.128, f32[2,16,256]{2,1,0:T(8,128)S(1)} %get-tuple-element.129, ...), kind=kOutput, calls=%fused_computation.20.clone.1 | convolution fusion | flops 90177536 | bytes 399364 | tf_op jit(solution)/shard_map/while/body/eval_jaxpr/gsrb,gsab->gra/dot_general | solution.py:54
  115.6 0.9 convolution_add_fusion
  (174 shorter events, 19.1 us)
Async XLA Ops:
  0.0 8.1 %copy-start = (bf16[8,64,256]{2,1,0:T(8,128)(2,1)S(1)}, bf16[8,64,256]{2,1,0:T(8,128)(2,1)}, u32[]{:S(2)}) copy-start(bf16[8,64,256]{2,1,0:T(8,128)(2,1)} %param.15) | copy-start | bytes 786436
  0.0 64.1 %copy-start.1 = (bf16[2,64,64]{2,1,0:T(8,128)(2,1)S(1)}, bf16[2,64,64]{2,1,0:T(8,128)(2,1)}, u32[]{:S(2)}) copy-start(bf16[2,64,64]{2,1,0:T(8,128)(2,1)} %param.19) | copy-start | bytes 49156
  0.0 67.2 %copy-start.6 = (s32[28,2]{0,1:T(2,128)S(1)}, s32[28,2]{0,1:T(2,128)}, u32[]{:S(2)}) copy-start(s32[28,2]{0,1:T(2,128)} %param.21) | copy-start | bytes 676
  0.0 67.4 %copy-start.8 = (bf16[4,64,64]{2,1,0:T(8,128)(2,1)S(1)}, bf16[4,64,64]{2,1,0:T(8,128)(2,1)}, u32[]{:S(2)}) copy-start(bf16[4,64,64]{2,1,0:T(8,128)(2,1)} %param.20) | copy-start | bytes 98308
  1.6 98.3 %collective-permute-start.1 = (bf16[8,19,256]{2,1,0:T(8,128)(2,1)S(1)}, bf16[8,19,256]{2,1,0:T(8,128)(2,1)S(1)}, u32[]{:S(2)}, u32[]{:S(2)}) collective-permute-start(bf16[8,19,256]{2,1,0:T(8,128)(2,1)S(1)} %copy_dynamic-update-slice_fusion), channel_id=1, source_target_pairs={{1,0},{2,1},{3,2},{4,3},{5,4},{6,5},{7,6},{8,7},{9,8},{10,9},{11,1... | collective-permute-start | bytes 233480 | tf_op jit(solution)/shard_map/ppermute | solution.py:23
  3.6 96.4 %collective-permute-start = (bf16[8,19,256]{2,1,0:T(8,128)(2,1)S(1)}, bf16[8,19,256]{2,1,0:T(8,128)(2,1)S(1)}, u32[]{:S(2)}, u32[]{:S(2)}) collective-permute-start(bf16[8,19,256]{2,1,0:T(8,128)(2,1)S(1)} %copy_dynamic-update-slice_fusion), channel_id=1, source_target_pairs={{0,1},{1,2},{2,3},{3,4},{4,5},{5,6},{6,7},{7,8},{8,9},{9,10},{10,1... | collective-permute-start | bytes 233480 | tf_op jit(solution)/shard_map/ppermute | solution.py:22
  12.7 66.9 %collective-permute-start.9 = (bf16[1,1024]{1,0:T(2,128)(2,1)}, bf16[1,1024]{1,0:T(2,128)(2,1)}, u32[]{:S(2)}, u32[]{:S(2)}) collective-permute-start(bf16[1,1024]{1,0:T(2,128)(2,1)} %reshape.428), channel_id=1, source_target_pairs={{1,0},{2,1},{3,2},{4,3},{5,4},{6,5},{7,6},{8,7},{9,8},{10,9},{11,1... | collective-permute-start | bytes 6152 | tf_op jit(solution)/shard_map/ppermute | solution.py:23
  14.7 66.9 %collective-permute-start.8 = (bf16[1,1024]{1,0:T(2,128)(2,1)}, bf16[1,1024]{1,0:T(2,128)(2,1)}, u32[]{:S(2)}, u32[]{:S(2)}) collective-permute-start(bf16[1,1024]{1,0:T(2,128)(2,1)} %reshape.428), channel_id=1, source_target_pairs={{0,1},{1,2},{2,3},{3,4},{4,5},{5,6},{6,7},{7,8},{8,9},{9,10},{10,1... | collective-permute-start | bytes 6152 | tf_op jit(solution)/shard_map/ppermute | solution.py:22
  19.0 66.6 %collective-permute-start.7 = (bf16[2,1024]{1,0:T(2,128)(2,1)}, bf16[2,1024]{1,0:T(2,128)(2,1)}, u32[]{:S(2)}, u32[]{:S(2)}) collective-permute-start(bf16[2,1024]{1,0:T(2,128)(2,1)} %reshape.425), channel_id=1, source_target_pairs={{1,0},{2,1},{3,2},{4,3},{5,4},{6,5},{7,6},{8,7},{9,8},{10,9},{11,1... | collective-permute-start | bytes 12296 | tf_op jit(solution)/shard_map/ppermute | solution.py:23
  71.2 3.3 %copy-start.7 = (s32[8,16]{1,0:T(8,128)S(1)}, s32[8,16]{1,0:T(8,128)}, u32[]{:S(2)}) copy-start(s32[8,16]{1,0:T(8,128)} %param.14) | copy-start | bytes 1540
  71.2 3.3 %copy-start.3 = (s32[15,8]{0,1:T(8,128)S(1)}, s32[15,8]{0,1:T(8,128)}, u32[]{:S(2)}) copy-start(s32[15,8]{0,1:T(8,128)} %param.18) | copy-start | bytes 1444
  71.9 5.4 %copy-start.4 = (bf16[8,3,256]{2,0,1:T(8,128)(2,1)S(1)}, bf16[8,3,256]{2,0,1:T(8,128)(2,1)}, u32[]{:S(2)}) copy-start(bf16[8,3,256]{2,0,1:T(8,128)(2,1)} %param.13) | copy-start | bytes 36868
  74.0 4.1 %slice-start = ((bf16[15,64,512]{2,1,0:T(8,128)(2,1)}), bf16[8,64,512]{2,1,0:T(8,128)(2,1)S(1)}, s32[]{:S(2)}) async-start(bf16[15,64,512]{2,1,0:T(8,128)(2,1)} %param.17), calls=%async_computation | async-start | bytes 1048576 | tf_op jit(solution)/shard_map/slice | solution.py:186
  78.0 0.9 slice-start.1
  78.0 1.2 %slice-start.2 = ((bf16[15,64,512]{2,1,0:T(8,128)(2,1)}), bf16[2,64,512]{2,1,0:T(8,128)(2,1)S(1)}, s32[]{:S(2)}) async-start(bf16[15,64,512]{2,1,0:T(8,128)(2,1)} %param.17), calls=%async_computation.2 | async-start | bytes 262144 | tf_op jit(solution)/shard_map/slice | solution.py:186
  78.0 1.4 %slice-start.3 = ((bf16[15,64,512]{2,1,0:T(8,128)(2,1)}), bf16[1,64,512]{2,1,0:T(8,128)(2,1)S(1)}, s32[]{:S(2)}) async-start(bf16[15,64,512]{2,1,0:T(8,128)(2,1)} %param.17), calls=%async_computation.3 | async-start | bytes 131072 | tf_op jit(solution)/shard_map/slice | solution.py:186
  79.0 13.4 %copy-start.2 = (bf16[14,64,64]{2,1,0:T(8,128)(2,1)S(1)}, bf16[14,64,64]{2,1,0:T(8,128)(2,1)}, u32[]{:S(2)}) copy-start(bf16[14,64,64]{2,1,0:T(8,128)(2,1)} %param.16) | copy-start | bytes 344068
  79.7 18.7 %copy-start.5 = (s32[1024]{0:T(1024)S(1)}, s32[1024]{0:T(1024)}, u32[]{:S(2)}) copy-start(s32[1024]{0:T(1024)} %pad_clamp_fusion.15) | copy-start | bytes 12292
  79.7 9.1 %collective-permute-start.6 = (bf16[2,1024]{1,0:T(2,128)(2,1)}, bf16[2,1024]{1,0:T(2,128)(2,1)S(1)}, u32[]{:S(2)}, u32[]{:S(2)}) collective-permute-start(bf16[2,1024]{1,0:T(2,128)(2,1)} %reshape.425), channel_id=1, source_target_pairs={{0,1},{1,2},{2,3},{3,4},{4,5},{5,6},{6,7},{7,8},{8,9},{9,10},{10,1... | collective-permute-start | bytes 12296 | tf_op jit(solution)/shard_map/ppermute | solution.py:22
  81.6 10.9 %collective-permute-start.5 = (bf16[4,1024]{1,0:T(4,128)(2,1)}, bf16[4,1024]{1,0:T(4,128)(2,1)S(1)}, u32[]{:S(2)}, u32[]{:S(2)}) collective-permute-start(bf16[4,1024]{1,0:T(4,128)(2,1)} %reshape.422), channel_id=1, source_target_pairs={{1,0},{2,1},{3,2},{4,3},{5,4},{6,5},{7,6},{8,7},{9,8},{10,9},{11,1... | collective-permute-start | bytes 24584 | tf_op jit(solution)/shard_map/ppermute | solution.py:23
  85.6 10.7 %collective-permute-start.4 = (bf16[4,1024]{1,0:T(4,128)(2,1)}, bf16[4,1024]{1,0:T(4,128)(2,1)S(1)}, u32[]{:S(2)}, u32[]{:S(2)}) collective-permute-start(bf16[4,1024]{1,0:T(4,128)(2,1)} %reshape.422), channel_id=1, source_target_pairs={{0,1},{1,2},{2,3},{3,4},{4,5},{5,6},{6,7},{7,8},{8,9},{9,10},{10,1... | collective-permute-start | bytes 24584 | tf_op jit(solution)/shard_map/ppermute | solution.py:22
  88.7 9.6 %collective-permute-start.3 = (bf16[8,1024]{1,0:T(8,128)(2,1)S(1)}, bf16[8,1024]{1,0:T(8,128)(2,1)S(1)}, u32[]{:S(2)}, u32[]{:S(2)}) collective-permute-start(bf16[8,1024]{1,0:T(8,128)(2,1)S(1)} %reshape.419), channel_id=1, source_target_pairs={{1,0},{2,1},{3,2},{4,3},{5,4},{6,5},{7,6},{8,7},{9,8},{10,9},{11,1... | collective-permute-start | bytes 49160 | tf_op jit(solution)/shard_map/ppermute | solution.py:23
  92.5 5.8 %collective-permute-start.2 = (bf16[8,1024]{1,0:T(8,128)(2,1)S(1)}, bf16[8,1024]{1,0:T(8,128)(2,1)S(1)}, u32[]{:S(2)}, u32[]{:S(2)}) collective-permute-start(bf16[8,1024]{1,0:T(8,128)(2,1)S(1)} %reshape.419), channel_id=1, source_target_pairs={{0,1},{1,2},{2,3},{3,4},{4,5},{5,6},{6,7},{7,8},{8,9},{9,10},{10,1... | collective-permute-start | bytes 49160 | tf_op jit(solution)/shard_map/ppermute | solution.py:22
where the time goes:
time: 117 us; the launch traced here: 116 us
  blocking collectives  42.6 us (36%)
  starting transfers between devices  27 us (23%)
  matrix products  23.2 us (20%)
  local copies, waits for them, and re-layouts  17.4 us (15%)
  other arithmetic  5.31 us (5%)
    all_gather x1, blocking collectives, gather_roots(): lax.all_gather(block_root.reshape(1, nrhs_count * rank_count), 'leaf', ax...  42.6 us
    ppermute x5, starting transfers between devices, with_halo(): before = lax.ppermute(last, axis, up)  16.9 us
    dot_general x4, matrix products, one_block(): jnp.einsum('gsrb,gsab->gra', sources[:, :, :nrhs_count, :], kernel_vals,...  14.1 us
    ppermute x5, starting transfers between devices, with_halo(): after = lax.ppermute(first, axis, down)  10.1 us
    gather x12, local copies, waits for them, and re-layouts, coarse_all(): upward[coarse][jnp.clip(node_ids + step_off, 0, node_count - 1)]  6.79 us
    dot_general x3, matrix products, shards(): jnp.einsum('crk,ckj->crj', levels[-1], transfer[starts[height]:starts[hei...  2.91 us
    gather x4, local copies, waits for them, and re-layouts, shards(): padded[located]  2.74 us
  transfers between devices with their start and end apart: 10, of which 0 were waited for; matrix products, arithmetic and copies ran while one was open for 24% of the time, Pallas kernels for 0%

commit v1 on v0

v1 whole, which is shorter than its diff:
```python
import functools

import jax
import jax.numpy as jnp
from jax import lax
from jax.experimental import pallas as pl
from jax.experimental.pallas import tpu as pltpu
from jax.sharding import PartitionSpec as P

KERNEL_SCALE = 0.01
SOFTENING = 0.05
F32 = jnp.float32
BF16 = jnp.bfloat16
NT = (((1,), (1,)), ((), ()))
MESH = pl.DeviceIdType.MESH


def dot(a, b):
    return jnp.dot(a, b, preferred_element_type=F32)


def dot_nt(a, b):
    return lax.dot_general(a, b, NT, preferred_element_type=F32)


def split3(s):
    hi = s.astype(BF16).astype(F32)
    rest = s - hi
    mid = rest.astype(BF16).astype(F32)
    return hi, mid, rest - mid


def source_rows(p):
    s = jnp.sum(p * p, axis=0, keepdims=True)
    ones = jnp.ones((3, p.shape[1]), F32)
    zeros = jnp.zeros((7, p.shape[1]), F32)
    return jnp.concatenate([p, *split3(s), ones, zeros], axis=0)


def target_rows(p):
    s = jnp.sum(p * p, axis=0, keepdims=True) + SOFTENING * SOFTENING
    ones = jnp.ones((3, p.shape[1]), F32)
    zeros = jnp.zeros((7, p.shape[1]), F32)
    return jnp.concatenate([-2.0 * p, ones, *split3(s), zeros], axis=0)


def twice(u):
    return jnp.concatenate([u, u], axis=1)


def body(
    n,
    charges,
    points,
    near_list,
    basis,
    transfer,
    coupling,
    far_list,
    top_transfer,
    top_coupling,
    top_list,
    out,
    src,
    rows,
    target,
    counts,
    nodes,
    roots,
    tops,
    near_send,
    near_recv,
    node_send,
    node_recv,
    root_send,
    root_recv,
):
    me = lax.axis_index("leaf")
    leaves, rhs, pts = charges.shape
    rank = basis.shape[1]
    depth = leaves.bit_length() - 1
    slots = 2 * leaves
    starts = [slots - 2 * (leaves >> h) for h in range(depth + 1)]
    levels_up = n.bit_length() - 3

    barrier = pltpu.get_barrier_semaphore()

    def greet(t, carry):
        other = lax.rem(me + t, n)
        pl.semaphore_signal(barrier, inc=1, device_id=(other,), device_id_type=MESH)
        return carry

    lax.fori_loop(1, n, greet, 0)

    for i in range(leaves):
        p = points[i].astype(F32)
        src[leaves + i, :rhs] = charges[i]
        src[leaves + i, rhs:] = source_rows(p).astype(BF16)
        target[i] = target_rows(p).astype(BF16)

    low = lax.broadcasted_iota(jnp.int32, (rhs, 2 * rank), 1) < rank

    for i in range(leaves):
        b = basis[i]
        nodes[slots + i] = dot_nt(charges[i], jnp.concatenate([b, b], axis=0)).astype(BF16)
    for h in range(depth):
        for q in range(leaves >> (h + 1)):
            c = starts[h] + 2 * q
            pair = jnp.where(low, nodes[slots + c], nodes[slots + c + 1])
            e = transfer[c : c + 2].reshape(2 * rank, rank)
            nodes[slots + starts[h + 1] + q] = twice(dot(pair, e)).astype(BF16)
    root = nodes[2 * slots - 2]
    nodes[2 * slots - 1] = root
    roots[me] = root

    pl.semaphore_wait(barrier, n - 1)

    def near_copy(right):
        return pltpu.make_async_remote_copy(
            src_ref=src.at[pl.ds(leaves, leaves)],
            dst_ref=src.at[pl.ds(0 if right else 2 * leaves, leaves)],
            send_sem=near_send.at[right],
            recv_sem=near_recv.at[right],
            device_id=(jnp.minimum(me + 1, n - 1) if right else jnp.maximum(me - 1, 0),),
            device_id_type=MESH,
        )

    def node_copy(right):
        return pltpu.make_async_remote_copy(
            src_ref=nodes.at[pl.ds(slots, slots)],
            dst_ref=nodes.at[pl.ds(0 if right else 2 * slots, slots)],
            send_sem=node_send.at[right],
            recv_sem=node_recv.at[right],
            device_id=(jnp.minimum(me + 1, n - 1) if right else jnp.maximum(me - 1, 0),),
            device_id_type=MESH,
        )

    @pl.when(me < n - 1)
    def _():
        near_copy(1).start()

    @pl.when(me > 0)
    def _():
        near_copy(0).start()

    def send_root(t, carry):
        pltpu.make_async_remote_copy(
            src_ref=nodes.at[2 * slots - 2],
            dst_ref=roots.at[me],
            send_sem=root_send,
            recv_sem=root_recv,
            device_id=(lax.rem(me + t, n),),
            device_id_type=MESH,
        ).start()
        return carry

    lax.fori_loop(1, n, send_root, 0)

    @pl.when(me < n - 1)
    def _():
        node_copy(1).start()

    @pl.when(me > 0)
    def _():
        node_copy(0).start()

    place = near_list[...] - (me - 1) * leaves
    leaf_id = lax.broadcasted_iota(jnp.int32, place.shape, 0)
    own = (place >= leaves) & (place < 2 * leaves)
    column = jnp.where(
        own, place - leaves, place - leaf_id + jnp.where(place < leaves, leaves, 0)
    )
    lane = lax.broadcasted_iota(jnp.int32, (leaves, 128), 1)
    total = jnp.zeros((leaves, 128), F32)
    for s in range(near_list.shape[1]):
        total = total + jnp.where(column[:, s : s + 1] == lane, 1.0, 0.0)
    counts[...] = total.reshape(leaves, 1, 128)

    def tile(source, goal, weight):
        d2 = dot(rows[source], goal)
        k = lax.rsqrt(d2).astype(BF16)
        w = jnp.broadcast_to(weight, (rhs, pts)).astype(BF16)
        return dot(src[source, :rhs] * w, k)

    def turn(i, carry):
        rows[i] = src[i, rhs:].astype(F32).T.astype(BF16)
        return carry

    lax.fori_loop(leaves, 2 * leaves, turn, 0)

    def own_leaf(i, carry):
        goal = target[i]
        weights = counts[i]
        acc = jnp.zeros((rhs, pts), F32)
        for j in range(leaves):
            acc = acc + tile(leaves + j, goal, weights[:, j : j + 1])
        out[i] = acc
        return carry

    lax.fori_loop(0, leaves, own_leaf, 0)

    @pl.when(me > 0)
    def _():
        near_copy(1).wait_recv()

    @pl.when(me == 0)
    def _():
        src[0:leaves] = src[leaves : 2 * leaves]

    @pl.when(me < n - 1)
    def _():
        near_copy(0).wait_recv()

    @pl.when(me == n - 1)
    def _():
        src[2 * leaves : 3 * leaves] = src[leaves : 2 * leaves]

    lax.fori_loop(0, leaves, turn, 0)
    lax.fori_loop(2 * leaves, 3 * leaves, turn, 0)

    def side_leaf(i, carry):
        goal = target[i]
        weights = counts[i]
        acc = out[i]
        for j in range(leaves + 1):
            source = i + j + leaves * ((i + j) // leaves)
            acc = acc + tile(source, goal, weights[:, leaves + j : leaves + j + 1])
        out[i] = acc
        return carry

    lax.fori_loop(0, leaves, side_leaf, 0)

    everyone = pltpu.make_async_remote_copy(
        src_ref=roots.at[pl.ds(0, n - 1)],
        dst_ref=roots.at[pl.ds(0, n - 1)],
        send_sem=root_send,
        recv_sem=root_recv,
        device_id=(lax.rem(me + 1, n),),
        device_id_type=MESH,
    )
    everyone.wait_recv()
    tt = top_transfer[...].reshape(2 * rank, rank)
    level = roots[...]
    for j in range(1, levels_up + 1):
        count = n >> j
        pairs = level.reshape(count, 2, rhs, 2 * rank)
        mixed = jnp.where(low[None], pairs[:, 0], pairs[:, 1]).reshape(count * rhs, 2 * rank)
        level = twice(dot(mixed, tt)).astype(BF16).reshape(count, rhs, 2 * rank)
        base = n - 2 * count
        tops[base : base + count] = level

    running = None
    for j in range(levels_up, 0, -1):
        count = n >> j
        base = n - 2 * count
        m = lax.shift_right_logical(me, j)
        p0 = top_list[base + m, 0]
        p1 = top_list[base + m, 1]
        k0 = jnp.clip(jnp.where(p0 < m, p0 - m + 2, p0 - m + 1), 0, 3)
        k1 = jnp.clip(jnp.where(p1 < m, p1 - m + 2, p1 - m + 1), 0, 3)
        p0 = jnp.clip(p0, 0, count - 1)
        p1 = jnp.clip(p1, 0, count - 1)
        pair = jnp.where(low, tops[base + p0], tops[base + p1])
        mats = jnp.concatenate([top_coupling[k0], top_coupling[k1]], axis=0)
        cross = dot(pair, mats)
        if running is not None:
            cross = cross + dot_nt(running.astype(BF16), top_transfer[lax.rem(m, 2)])
        running = cross
    running = dot_nt(running.astype(BF16), top_transfer[lax.rem(me, 2)])

    @pl.when(me > 0)
    def _():
        node_copy(1).wait_recv()

    @pl.when(me < n - 1)
    def _():
        node_copy(0).wait_recv()

    def couple(h, q):
        row = starts[h] + q
        width = depth - h

        def fetch(s):
            at = far_list[row, s] - (me - 1) * (leaves >> h)
            block = lax.shift_right_logical(jnp.clip(at, 0, (3 * leaves >> h) - 1), width)
            inner = lax.bitwise_and(at, (leaves >> h) - 1)
            return nodes[block * slots + starts[h] + inner]

        wide = [jnp.where(low, fetch(s), fetch(s + 1)) for s in range(0, far_list.shape[1], 2)]
        return dot_nt(jnp.concatenate(wide, axis=1), coupling[row])

    back = [couple(depth, 0) + running]
    for h in range(depth - 1, -1, -1):
        below = []
        for q in range(leaves >> (h + 1)):
            c = starts[h] + 2 * q
            e = transfer[c : c + 2].reshape(2 * rank, rank)
            pushed = dot_nt(back[q].astype(BF16), e)
            below.append(couple(h, 2 * q) + pushed[:, :rank])
            below.append(couple(h, 2 * q + 1) + pushed[:, rank:])
        back = below
    for i in range(leaves):
        out[i] = KERNEL_SCALE * out[i] + dot(back[i].astype(BF16), basis[i])

    everyone.wait_send()

    @pl.when(me < n - 1)
    def _():
        near_copy(1).wait_send()
        node_copy(1).wait_send()

    @pl.when(me > 0)
    def _():
        near_copy(0).wait_send()
        node_copy(0).wait_send()


def solution(mesh):
    n = mesh.shape["leaf"]
    placed = (
        P("leaf", None, None),
        P("leaf", None, None),
        P("leaf", None),
        P("leaf", None, None),
        P("leaf", None, None),
        P("leaf", None, None),
        P("leaf", None),
        P(),
        P(),
        P(),
    )

    def shards(*args):
        leaves, rhs, pts = args[0].shape
        rank = args[3].shape[1]
        slots = 2 * leaves
        vmem = pl.BlockSpec(memory_space=pltpu.VMEM)
        smem = pl.BlockSpec(memory_space=pltpu.SMEM)
        dma = pltpu.SemaphoreType.DMA
        return pl.pallas_call(
            functools.partial(body, n),
            out_shape=jax.ShapeDtypeStruct((leaves, rhs, pts), F32),
            in_specs=[vmem, vmem, vmem, vmem, vmem, vmem, smem, vmem, vmem, smem],
            out_specs=vmem,
            scratch_shapes=[
                pltpu.VMEM((3 * leaves, 2 * rhs, pts), BF16),
                pltpu.VMEM((3 * leaves, pts, 16), BF16),
                pltpu.VMEM((leaves, 16, pts), BF16),
                pltpu.VMEM((leaves, 1, 128), F32),
                pltpu.VMEM((3 * slots, rhs, 2 * rank), BF16),
                pltpu.VMEM((n, rhs, 2 * rank), BF16),
                pltpu.VMEM((n, rhs, 2 * rank), BF16),
                dma((2,)),
                dma((2,)),
                dma((2,)),
                dma((2,)),
                dma(()),
                dma(()),
            ],
            compiler_params=pltpu.CompilerParams(
                collective_id=0, has_side_effects=True, vmem_limit_bytes=40 * 1024 * 1024
            ),
        )(*args)

    return jax.shard_map(
        shards, mesh=mesh, in_specs=placed, out_specs=P("leaf", None, None), check_vma=False
    )
```

time: 117 us -> 37.8 us (0.32)
  blocking collectives: 42.6 us -> 0 us
  Pallas kernels: 0 us -> 29.5 us
  starting transfers between devices: 27 us -> 0 us
  matrix products: 23.2 us -> 0 us
  local copies, waits for them, and re-layouts: 17.4 us -> 7.61 us
  other arithmetic: 5.31 us -> 0 us
    all_gather x1 -> x0, blocking collectives: 42.6 us -> none  [gather_roots(): lax.all_gather(block_root.reshape(1, nrhs_count * rank_count), 'leaf', ax...]
    pallas_call x0 -> x1, Pallas kernels: none -> 29.5 us  [shards(): pl.pallas_call(functools.partial(body, n), out_shape=jax.ShapeDtypeStruct...]
    ppermute x10 -> x0, starting transfers between devices: 27 us -> none  [the longest x5 16.9 us: with_halo(): before = lax.ppermute(last, axis, up)]
    dot_general x31 -> x0, matrix products: 23.2 us -> none  [the longest x4 14.1 us: one_block(): jnp.einsum('gsrb,gsab->gra', sources[:, :, :nrhs_count, :], kernel_vals,...]
    gather x17 -> x0, local copies, waits for them, and re-layouts: 10.2 us -> none  [the longest x12 6.79 us: coarse_all(): upward[coarse][jnp.clip(node_ids + step_off, 0, node_count - 1)]]
    unnamed x20, local copies, waits for them, and re-layouts: 1.01 us -> 7.61 us
    reshape x13 -> x0, local copies, waits for them, and re-layouts: 3.83 us -> none  [the longest x4 2.15 us: shards(): tier.reshape(tier.shape[0], nrhs_count * rank_count)]
    concatenate x5 -> x0, other arithmetic: 2.19 us -> none  [with_halo(): value = jnp.concatenate([before, value, after], axis=dim)]
  transfers between devices with their start and end apart: 10 -> 0, of which waited for: 0 -> 0; matrix products, arithmetic and copies ran while one was open for 24% -> 0% of each run, Pallas kernels for 0% -> 0%
where the time goes in v1:
time: 37.8 us; the launch traced here: 37.1 us
  Pallas kernels  29.5 us (78%)
  local copies, waits for them, and re-layouts  7.61 us (20%)
    pallas_call x1, Pallas kernels, shards(): pl.pallas_call(functools.partial(body, n), out_shape=jax.ShapeDtypeStruct...  29.5 us
    unnamed x20, local copies, waits for them, and re-layouts  7.61 us

profile of v1, /device:TPU:1, one launch (start us, length us, event | category | flops | bytes accessed | tf_op | source)
XLA Modules:
  0.0 37.1 jit_solution(10285694744603778003)
XLA Ops:
  0.0 0.0 copy-start.5
  0.0 0.8 %copy.12.far_list = s32[15,8]{1,0:T(8,128)S(1)} copy(s32[15,8]{0,1:T(8,128)} %param.16) | data formatting | bytes 960 | tf_op args[6]
  0.8 0.0 copy-start.7
  0.8 0.7 %copy.11.points = bf16[8,3,256]{2,1,0:T(4,128)(2,1)S(1)} copy(bf16[8,3,256]{2,0,1:T(8,128)(2,1)} %param.11) | data formatting | bytes 24576 | tf_op args[1]
  1.5 0.0 copy-done.7
  1.5 0.0 copy-start.6
  1.5 0.1 copy.13.top_list
  1.6 0.0 copy-done.5
  1.6 0.6 %copy-done.6 = s32[8,16]{1,0:T(8,128)S(1)} copy-done((s32[8,16]{1,0:T(8,128)S(1)}, s32[8,16]{1,0:T(8,128)}, u32[]{:S(2)}) %copy-start.6) | copy-done | bytes 536
  2.2 0.0 copy-start
  2.2 1.2 %copy-done = bf16[15,64,512]{2,1,0:T(8,128)(2,1)S(1)} copy-done((bf16[15,64,512]{2,1,0:T(8,128)(2,1)S(1)}, bf16[15,64,512]{2,1,0:T(8,128)(2,1)}, u32[]{:S(2)}) %copy-start) | copy-done | bytes 983064
  3.4 0.0 copy-start.1
  3.4 0.9 %copy-done.1 = bf16[8,64,256]{2,1,0:T(8,128)(2,1)S(1)} copy-done((bf16[8,64,256]{2,1,0:T(8,128)(2,1)S(1)}, bf16[8,64,256]{2,1,0:T(8,128)(2,1)}, u32[]{:S(2)}) %copy-start.1) | copy-done | bytes 262168
  4.4 0.0 copy-start.2
  4.4 0.9 %copy-done.2 = bf16[14,64,64]{2,1,0:T(8,128)(2,1)S(1)} copy-done((bf16[14,64,64]{2,1,0:T(8,128)(2,1)S(1)}, bf16[14,64,64]{2,1,0:T(8,128)(2,1)}, u32[]{:S(2)}) %copy-start.2) | copy-done | bytes 114712
  5.3 0.0 copy-start.3
  5.3 0.8 %copy-done.3 = bf16[8,16,256]{2,1,0:T(8,128)(2,1)S(1)} copy-done((bf16[8,16,256]{2,1,0:T(8,128)(2,1)S(1)}, bf16[8,16,256]{2,1,0:T(8,128)(2,1)}, u32[]{:S(2)}) %copy-start.3) | copy-done | bytes 65560
  6.1 0.0 copy-start.4
  6.1 0.8 %copy-done.4 = bf16[4,64,64]{2,1,0:T(8,128)(2,1)S(1)} copy-done((bf16[4,64,64]{2,1,0:T(8,128)(2,1)S(1)}, bf16[4,64,64]{2,1,0:T(8,128)(2,1)}, u32[]{:S(2)}) %copy-start.4) | copy-done | bytes 32792
  7.0 29.5 %shard_map.100 = f32[8,16,256]{2,1,0:T(8,128)S(1)} custom-call(bf16[8,16,256]{2,1,0:T(8,128)(2,1)S(1)} %copy-done.3, bf16[8,3,256]{2,1,0:T(4,128)(2,1)S(1)} %copy.11.points, s32[8,16]{1,0:T(8,128)S(1)} %copy-done.6, bf16[8,64,256]{2,1,0:T(8,128)(2,1)S(1)} %copy-done.1, bf16[14,64,64]{2,1,0:T(8,128)(2,1)S(1)} %copy-done.2, bf16[15,64,512]{2,1,0:T(8,128)(2,1)S(1)} %copy-done, ...), custom_call_target="tpu_custom_call" | custom-call | tf_op jit(solution)/shard_map/pallas_call | solution.py:340
  36.4 0.7 %copy.15 = f32[8,16,256]{2,1,0:T(8,128)} copy(f32[8,16,256]{2,1,0:T(8,128)S(1)} %shard_map.100) | data formatting | bytes 262144
Async XLA Ops:
  0.0 1.6 %copy-start.5 = (bf16[2,64,64]{2,1,0:T(8,128)(2,1)S(1)}, bf16[2,64,64]{2,1,0:T(8,128)(2,1)}, u32[]{:S(2)}) copy-start(bf16[2,64,64]{2,1,0:T(8,128)(2,1)} %top_transfer.1) | copy-start | bytes 49156
  0.8 0.7 %copy-start.7 = (s32[28,2]{0,1:T(2,128)S(1)}, s32[28,2]{0,1:T(2,128)}, u32[]{:S(2)}) copy-start(s32[28,2]{0,1:T(2,128)} %param.19) | copy-start | bytes 676
  1.5 0.7 %copy-start.6 = (s32[8,16]{1,0:T(8,128)S(1)}, s32[8,16]{1,0:T(8,128)}, u32[]{:S(2)}) copy-start(s32[8,16]{1,0:T(8,128)} %near_list.1) | copy-start | bytes 1540
  2.2 1.2 %copy-start = (bf16[15,64,512]{2,1,0:T(8,128)(2,1)S(1)}, bf16[15,64,512]{2,1,0:T(8,128)(2,1)}, u32[]{:S(2)}) copy-start(bf16[15,64,512]{2,1,0:T(8,128)(2,1)} %coupling.1) | copy-start | bytes 2949124
  3.4 0.9 %copy-start.1 = (bf16[8,64,256]{2,1,0:T(8,128)(2,1)S(1)}, bf16[8,64,256]{2,1,0:T(8,128)(2,1)}, u32[]{:S(2)}) copy-start(bf16[8,64,256]{2,1,0:T(8,128)(2,1)} %basis.1) | copy-start | bytes 786436
  4.4 0.9 %copy-start.2 = (bf16[14,64,64]{2,1,0:T(8,128)(2,1)S(1)}, bf16[14,64,64]{2,1,0:T(8,128)(2,1)}, u32[]{:S(2)}) copy-start(bf16[14,64,64]{2,1,0:T(8,128)(2,1)} %transfer.1) | copy-start | bytes 344068
  5.3 0.8 %copy-start.3 = (bf16[8,16,256]{2,1,0:T(8,128)(2,1)S(1)}, bf16[8,16,256]{2,1,0:T(8,128)(2,1)}, u32[]{:S(2)}) copy-start(bf16[8,16,256]{2,1,0:T(8,128)(2,1)} %charges.1) | copy-start | bytes 196612
  6.1 0.8 %copy-start.4 = (bf16[4,64,64]{2,1,0:T(8,128)(2,1)S(1)}, bf16[4,64,64]{2,1,0:T(8,128)(2,1)}, u32[]{:S(2)}) copy-start(bf16[4,64,64]{2,1,0:T(8,128)(2,1)} %top_coupling.1) | copy-start | bytes 98308

commit v2 on v1

--- a/solution.py
+++ b/solution.py
@@ -51,6 +51,16 @@
 def body(
     n,
     charges,
+    points_hbm,
+    near_list_hbm,
+    basis_hbm,
+    transfer_hbm,
+    coupling_hbm,
+    far_list_hbm,
+    top_transfer_hbm,
+    top_coupling_hbm,
+    top_list_hbm,
+    out,
     points,
     near_list,
     basis,
@@ -60,7 +70,7 @@
     top_transfer,
     top_coupling,
     top_list,
-    out,
+    load_sem,
     src,
     rows,
     target,
@@ -92,17 +102,38 @@
 
     lax.fori_loop(1, n, greet, 0)
 
+    loads = {}
+    for at, (name, origin, place) in enumerate(
+        (
+            ("basis", basis_hbm, basis),
+            ("charges", charges, src.at[pl.ds(2 * leaves, leaves), pl.ds(0, rhs)]),
+            ("points", points_hbm, points),
+            ("transfer", transfer_hbm, transfer),
+            ("near_list", near_list_hbm, near_list),
+            ("top_transfer", top_transfer_hbm, top_transfer),
+            ("top_coupling", top_coupling_hbm, top_coupling),
+            ("top_list", top_list_hbm, top_list),
+            ("far_list", far_list_hbm, far_list),
+            ("coupling", coupling_hbm, coupling),
+        )
+    ):
+        loads[name] = pltpu.make_async_copy(origin, place, load_sem.at[at])
+        loads[name].start()
+
+    loads["points"].wait()
+    loads["charges"].wait()
     for i in range(leaves):
-        p = points[i].astype(F32)
-        src[leaves + i, :rhs] = charges[i]
-        src[leaves + i, rhs:] = source_rows(p).astype(BF16)
+        p = points[:, i].astype(F32)
+        src[2 * leaves + i, rhs:] = source_rows(p).astype(BF16)
         target[i] = target_rows(p).astype(BF16)
 
     low = lax.broadcasted_iota(jnp.int32, (rhs, 2 * rank), 1) < rank
 
+    loads["basis"].wait()
+    loads["transfer"].wait()
     for i in range(leaves):
         b = basis[i]
-        nodes[slots + i] = dot_nt(charges[i], jnp.concatenate([b, b], axis=0)).astype(BF16)
+        nodes[slots + i] = dot_nt(src[2 * leaves + i, :rhs], jnp.concatenate([b, b], axis=0)).astype(BF16)
     for h in range(depth):
         for q in range(leaves >> (h + 1)):
             c = starts[h] + 2 * q
@@ -117,8 +148,8 @@
 
     def near_copy(right):
         return pltpu.make_async_remote_copy(
-            src_ref=src.at[pl.ds(leaves, leaves)],
-            dst_ref=src.at[pl.ds(0 if right else 2 * leaves, leaves)],
+            src_ref=src.at[pl.ds(2 * leaves, leaves)],
+            dst_ref=src.at[pl.ds(0 if right else leaves, leaves)],
             send_sem=near_send.at[right],
             recv_sem=near_recv.at[right],
             device_id=(jnp.minimum(me + 1, n - 1) if right else jnp.maximum(me - 1, 0),),
@@ -163,6 +194,8 @@
     @pl.when(me > 0)
     def _():
         node_copy(0).start()
+
+    loads["near_list"].wait()
 
     place = near_list[...] - (me - 1) * leaves
     leaf_id = lax.broadcasted_iota(jnp.int32, place.shape, 0)
@@ -176,25 +209,23 @@
         total = total + jnp.where(column[:, s : s + 1] == lane, 1.0, 0.0)
     counts[...] = total.reshape(leaves, 1, 128)
 
-    def tile(source, goal, weight):
-        d2 = dot(rows[source], goal)
+    def tiles(first, count, goal, weights):
+        d2 = dot(rows[pl.ds(first, count)].reshape(count * pts, 16), goal)
         k = lax.rsqrt(d2).astype(BF16)
-        w = jnp.broadcast_to(weight, (rhs, pts)).astype(BF16)
-        return dot(src[source, :rhs] * w, k)
+        scaled = [
+            src[first + j, :rhs] * jnp.broadcast_to(weights[:, j : j + 1], (rhs, pts)).astype(BF16)
+            for j in range(count)
+        ]
+        return dot(jnp.concatenate(scaled, axis=1), k)
 
     def turn(i, carry):
         rows[i] = src[i, rhs:].astype(F32).T.astype(BF16)
         return carry
 
-    lax.fori_loop(leaves, 2 * leaves, turn, 0)
+    lax.fori_loop(2 * leaves, 3 * leaves, turn, 0)
 
     def own_leaf(i, carry):
-        goal = target[i]
-        weights = counts[i]
-        acc = jnp.zeros((rhs, pts), F32)
-        for j in range(leaves):
-            acc = acc + tile(leaves + j, goal, weights[:, j : j + 1])
-        out[i] = acc
+        out[i] = tiles(2 * leaves, leaves, target[i], counts[i])
         return carry
 
     lax.fori_loop(0, leaves, own_leaf, 0)
@@ -205,7 +236,7 @@
 
     @pl.when(me == 0)
     def _():
-        src[0:leaves] = src[leaves : 2 * leaves]
+        src[0:leaves] = src[2 * leaves : 3 * leaves]
 
     @pl.when(me < n - 1)
     def _():
@@ -213,19 +244,13 @@
 
     @pl.when(me == n - 1)
     def _():
-        src[2 * leaves : 3 * leaves] = src[leaves : 2 * leaves]
-
-    lax.fori_loop(0, leaves, turn, 0)
-    lax.fori_loop(2 * leaves, 3 * leaves, turn, 0)
+        src[leaves : 2 * leaves] = src[2 * leaves : 3 * leaves]
+
+    lax.fori_loop(0, 2 * leaves, turn, 0)
 
     def side_leaf(i, carry):
-        goal = target[i]
-        weights = counts[i]
-        acc = out[i]
-        for j in range(leaves + 1):
-            source = i + j + leaves * ((i + j) // leaves)
-            acc = acc + tile(source, goal, weights[:, leaves + j : leaves + j + 1])
-        out[i] = acc
+        weights = counts[i][:, leaves:]
+        out[i] = out[i] + tiles(i, leaves + 1, target[i], weights)
         return carry
 
     lax.fori_loop(0, leaves, side_leaf, 0)
@@ -239,6 +264,8 @@
         device_id_type=MESH,
     )
     everyone.wait_recv()
+    for name in ("top_transfer", "top_coupling", "top_list", "far_list", "coupling"):
+        loads[name].wait()
     tt = top_transfer[...].reshape(2 * rank, rank)
     level = roots[...]
     for j in range(1, levels_up + 1):
@@ -254,8 +281,8 @@
         count = n >> j
         base = n - 2 * count
         m = lax.shift_right_logical(me, j)
-        p0 = top_list[base + m, 0]
-        p1 = top_list[base + m, 1]
+        p0 = top_list[0, base + m]
+        p1 = top_list[1, base + m]
         k0 = jnp.clip(jnp.where(p0 < m, p0 - m + 2, p0 - m + 1), 0, 3)
         k1 = jnp.clip(jnp.where(p1 < m, p1 - m + 2, p1 - m + 1), 0, 3)
         p0 = jnp.clip(p0, 0, count - 1)
@@ -281,12 +308,12 @@
         width = depth - h
 
         def fetch(s):
-            at = far_list[row, s] - (me - 1) * (leaves >> h)
+            at = far_list[s, row] - (me - 1) * (leaves >> h)
             block = lax.shift_right_logical(jnp.clip(at, 0, (3 * leaves >> h) - 1), width)
             inner = lax.bitwise_and(at, (leaves >> h) - 1)
             return nodes[block * slots + starts[h] + inner]
 
-        wide = [jnp.where(low, fetch(s), fetch(s + 1)) for s in range(0, far_list.shape[1], 2)]
+        wide = [jnp.where(low, fetch(s), fetch(s + 1)) for s in range(0, far_list.shape[0], 2)]
         return dot_nt(jnp.concatenate(wide, axis=1), coupling[row])
 
     back = [couple(depth, 0) + running]
@@ -330,19 +357,51 @@
         P(),
     )
 
-    def shards(*args):
-        leaves, rhs, pts = args[0].shape
-        rank = args[3].shape[1]
+    def shards(
+        charges,
+        points,
+        near_list,
+        basis,
+        transfer,
+        coupling,
+        far_list,
+        top_transfer,
+        top_coupling,
+        top_list,
+    ):
+        args = (
+            charges,
+            jnp.transpose(points, (1, 0, 2)),
+            near_list,
+            basis,
+            transfer,
+            coupling,
+            far_list.T,
+            top_transfer,
+            top_coupling,
+            top_list.T,
+        )
+        leaves, rhs, pts = charges.shape
+        rank = basis.shape[1]
         slots = 2 * leaves
         vmem = pl.BlockSpec(memory_space=pltpu.VMEM)
-        smem = pl.BlockSpec(memory_space=pltpu.SMEM)
+        hbm = pl.BlockSpec(memory_space=pltpu.HBM)
+
+        def held(kind, array):
+            return kind(array.shape, array.dtype)
+
         dma = pltpu.SemaphoreType.DMA
         return pl.pallas_call(
             functools.partial(body, n),
             out_shape=jax.ShapeDtypeStruct((leaves, rhs, pts), F32),
-            in_specs=[vmem, vmem, vmem, vmem, vmem, vmem, smem, vmem, vmem, smem],
+            in_specs=[hbm] * len(args),
             out_specs=vmem,
             scratch_shapes=[
+                *(
+                    held(pltpu.SMEM if at in (6, 9) else pltpu.VMEM, args[at])
+                    for at in range(1, len(args))
+                ),
+                dma((len(args),)),
                 pltpu.VMEM((3 * leaves, 2 * rhs, pts), BF16),
                 pltpu.VMEM((3 * leaves, pts, 16), BF16),
                 pltpu.VMEM((leaves, 16, pts), BF16),
@@ -358,7 +417,7 @@
                 dma(()),
             ],
             compiler_params=pltpu.CompilerParams(
-                collective_id=0, has_side_effects=True, vmem_limit_bytes=40 * 1024 * 1024
+                collective_id=0, has_side_effects=True, vmem_limit_bytes=63 * 1024 * 1024
             ),
         )(*args)
 

time: 37.8 us -> 26.2 us (0.69)
  local copies, waits for them, and re-layouts: 7.61 us -> 1.57 us
  Pallas kernels: 29.5 us -> 24.2 us
    unnamed x20 -> x1, local copies, waits for them, and re-layouts: 7.61 us -> 1.57 us
    pallas_call x1, Pallas kernels: 29.5 us -> 24.2 us  [shards(): pl.pallas_call(functools.partial(body, n), out_shape=jax.ShapeDtypeStruct...]
where the time goes in v2:
time: 26.2 us; the launch traced here: 25.8 us
  Pallas kernels  24.2 us (92%)
  local copies, waits for them, and re-layouts  1.57 us (6%)
    pallas_call x1, Pallas kernels, shards(): pl.pallas_call(functools.partial(body, n), out_shape=jax.ShapeDtypeStruct...  24.2 us
    unnamed x1, local copies, waits for them, and re-layouts  1.57 us

profile of v2, /device:TPU:1, one launch (start us, length us, event | category | flops | bytes accessed | tf_op | source)
XLA Modules:
  0.0 25.8 jit_solution(4399194886788827274)
XLA Ops:
  0.0 24.2 %shard_map.100 = f32[8,16,256]{2,1,0:T(8,128)} custom-call(bf16[8,16,256]{2,1,0:T(8,128)(2,1)} %charges.1, bf16[3,8,256]{2,1,0:T(8,128)(2,1)} %bitcast.3, s32[8,16]{1,0:T(8,128)} %near_list_hbm.1, bf16[8,64,256]{2,1,0:T(8,128)(2,1)} %basis_hbm.1, bf16[14,64,64]{2,1,0:T(8,128)(2,1)} %transfer_hbm.1, bf16[15,64,512]{2,1,0:T(8,128)(2,1)} %coupling_hbm.1, ...), custom_call_target="tpu_custom_call" | custom-call | tf_op jit(solution)/shard_map/pallas_call | solution.py:394
  24.2 1.6 %copy.12 = f32[8,16,256]{2,1,0:T(8,128)} copy(f32[8,16,256]{2,1,0:T(8,128)} %shard_map.100) | data formatting | bytes 262144

commit v3 on v2

--- a/solution.py
+++ b/solution.py
@@ -210,25 +210,30 @@
     counts[...] = total.reshape(leaves, 1, 128)
 
     def tiles(first, count, goal, weights):
-        d2 = dot(rows[pl.ds(first, count)].reshape(count * pts, 16), goal)
-        k = lax.rsqrt(d2).astype(BF16)
         scaled = [
             src[first + j, :rhs] * jnp.broadcast_to(weights[:, j : j + 1], (rhs, pts)).astype(BF16)
             for j in range(count)
         ]
-        return dot(jnp.concatenate(scaled, axis=1), k)
+        total = None
+        for j in range(0, count, 3):
+            some = min(3, count - j)
+            d2 = dot(rows[pl.ds(first + j, some)].reshape(some * pts, 16), goal)
+            k = lax.rsqrt(d2).astype(BF16)
+            part = dot(jnp.concatenate(scaled[j : j + some], axis=1), k)
+            total = part if total is None else total + part
+        return total
 
     def turn(i, carry):
         rows[i] = src[i, rhs:].astype(F32).T.astype(BF16)
         return carry
 
-    lax.fori_loop(2 * leaves, 3 * leaves, turn, 0)
+    lax.fori_loop(2 * leaves, 3 * leaves, turn, 0, unroll=8)
 
     def own_leaf(i, carry):
         out[i] = tiles(2 * leaves, leaves, target[i], counts[i])
         return carry
 
-    lax.fori_loop(0, leaves, own_leaf, 0)
+    lax.fori_loop(0, leaves, own_leaf, 0, unroll=2)
 
     @pl.when(me > 0)
     def _():
@@ -246,14 +251,14 @@
     def _():
         src[leaves : 2 * leaves] = src[2 * leaves : 3 * leaves]
 
-    lax.fori_loop(0, 2 * leaves, turn, 0)
+    lax.fori_loop(0, 2 * leaves, turn, 0, unroll=8)
 
     def side_leaf(i, carry):
         weights = counts[i][:, leaves:]
         out[i] = out[i] + tiles(i, leaves + 1, target[i], weights)
         return carry
 
-    lax.fori_loop(0, leaves, side_leaf, 0)
+    lax.fori_loop(0, leaves, side_leaf, 0, unroll=2)
 
     everyone = pltpu.make_async_remote_copy(
         src_ref=roots.at[pl.ds(0, n - 1)],

time: 26.2 us -> 21.7 us (0.83); the launches traced: 25.8 us -> 21.5 us
  Pallas kernels: 24.2 us -> 20 us
    pallas_call x1, Pallas kernels: 24.2 us -> 20 us  [shards(): pl.pallas_call(functools.partial(body, n), out_shape=jax.ShapeDtypeStruct...]
where the time goes in v3:
time: 21.7 us; the launch traced here: 21.5 us
  Pallas kernels  20 us (92%)
  local copies, waits for them, and re-layouts  1.57 us (7%)
    pallas_call x1, Pallas kernels, shards(): pl.pallas_call(functools.partial(body, n), out_shape=jax.ShapeDtypeStruct...  20 us
    unnamed x1, local copies, waits for them, and re-layouts  1.57 us

profile of v3, /device:TPU:1, one launch (start us, length us, event | category | flops | bytes accessed | tf_op | source)
XLA Modules:
  0.0 21.5 jit_solution(14198136991818632316)
XLA Ops:
  0.0 20.0 %shard_map.100 = f32[8,16,256]{2,1,0:T(8,128)} custom-call(bf16[8,16,256]{2,1,0:T(8,128)(2,1)} %charges.1, bf16[3,8,256]{2,1,0:T(8,128)(2,1)} %bitcast.3, s32[8,16]{1,0:T(8,128)} %near_list_hbm.1, bf16[8,64,256]{2,1,0:T(8,128)(2,1)} %basis_hbm.1, bf16[14,64,64]{2,1,0:T(8,128)(2,1)} %transfer_hbm.1, bf16[15,64,512]{2,1,0:T(8,128)(2,1)} %coupling_hbm.1, ...), custom_call_target="tpu_custom_call" | custom-call | tf_op jit(solution)/shard_map/pallas_call | solution.py:399
  20.0 1.6 %copy.12 = f32[8,16,256]{2,1,0:T(8,128)} copy(f32[8,16,256]{2,1,0:T(8,128)} %shard_map.100) | data formatting | bytes 262144

commit v4 on v3

--- a/solution.py
+++ b/solution.py
@@ -233,7 +233,7 @@
         out[i] = tiles(2 * leaves, leaves, target[i], counts[i])
         return carry
 
-    lax.fori_loop(0, leaves, own_leaf, 0, unroll=2)
+    lax.fori_loop(0, leaves, own_leaf, 0, unroll=4)
 
     @pl.when(me > 0)
     def _():
@@ -258,7 +258,7 @@
         out[i] = out[i] + tiles(i, leaves + 1, target[i], weights)
         return carry
 
-    lax.fori_loop(0, leaves, side_leaf, 0, unroll=2)
+    lax.fori_loop(0, leaves, side_leaf, 0, unroll=4)
 
     everyone = pltpu.make_async_remote_copy(
         src_ref=roots.at[pl.ds(0, n - 1)],

time: 21.7 us -> 21.4 us (0.986)
  Pallas kernels: 20 us -> 19.7 us
    pallas_call x1, Pallas kernels: 20 us -> 19.7 us  [shards(): pl.pallas_call(functools.partial(body, n), out_shape=jax.ShapeDtypeStruct...]
where the time goes in v4:
time: 21.4 us; the launch traced here: 21.3 us
  Pallas kernels  19.7 us (92%)
  local copies, waits for them, and re-layouts  1.57 us (7%)
    pallas_call x1, Pallas kernels, shards(): pl.pallas_call(functools.partial(body, n), out_shape=jax.ShapeDtypeStruct...  19.7 us
    unnamed x1, local copies, waits for them, and re-layouts  1.57 us

profile of v4, /device:TPU:1, one launch (start us, length us, event | category | flops | bytes accessed | tf_op | source)
XLA Modules:
  0.0 21.3 jit_solution(9434648598769500329)
XLA Ops:
  0.0 19.7 %shard_map.100 = f32[8,16,256]{2,1,0:T(8,128)} custom-call(bf16[8,16,256]{2,1,0:T(8,128)(2,1)} %charges.1, bf16[3,8,256]{2,1,0:T(8,128)(2,1)} %bitcast.3, s32[8,16]{1,0:T(8,128)} %near_list_hbm.1, bf16[8,64,256]{2,1,0:T(8,128)(2,1)} %basis_hbm.1, bf16[14,64,64]{2,1,0:T(8,128)(2,1)} %transfer_hbm.1, bf16[15,64,512]{2,1,0:T(8,128)(2,1)} %coupling_hbm.1, ...), custom_call_target="tpu_custom_call" | custom-call | tf_op jit(solution)/shard_map/pallas_call | solution.py:399
  19.7 1.6 %copy.12 = f32[8,16,256]{2,1,0:T(8,128)} copy(f32[8,16,256]{2,1,0:T(8,128)} %shard_map.100) | data formatting | bytes 262144
